TPU v7x, 128 devices: a whole 4x4x4 slice. The times are simulated.
128 devices in a mesh: dp: 32 (over x, y, z_lo), mp: 4 (over z_hi, core).
Axes of the slice: x: 4, y: 4, z: 4 (z_hi: 2, z_lo: 2; z = z_hi * 2 + z_lo), core: 2. Of those that a mesh axis runs over, the one named last changes fastest.
Arguments:
- hidden: bfloat16 [6144, 5120], P('dp'), may hold values from -14 to 14
- w_query: bfloat16 [5120, 4096], P('dp', 'mp'), may hold values from -0.15625 to 0.15625
- w_key: bfloat16 [5120, 512], P('dp', 'mp'), may hold values from -0.078125 to 0.078125
- w_value: bfloat16 [5120, 512], P('dp', 'mp'), may hold values from -0.078125 to 0.078125
- out_grad: bfloat16 [6144, 4096], P('dp', 'mp'), may hold values from -6 to 6
- lengths: int32 [4], replicated, may hold values from 1 to 5376, 6144 in all
- advantages: float32 [4], replicated, may hold values from -4 to 4
Outputs:
- attended: bfloat16 [6144, 4096], P('dp', 'mp')
- grad_hidden: bfloat16 [6144, 5120], P('dp', 'mp')
- grad_w_query: bfloat16 [5120, 4096], P('dp', 'mp')
- grad_w_key: bfloat16 [5120, 512], P('dp', 'mp')
- grad_w_value: bfloat16 [5120, 512], P('dp', 'mp')
Inputs may be any that keep to these rules, and one draw needn't show every extreme that they name: Response r occupies the next lengths[r] tokens of the stream, in order; the lengths sum to 6144.
All inputs are finite; a program needn't handle non-finite values.
Results may differ from a plain program's by a relative error of at most 0.039.
Values may be sent and summed in bfloat16 or wider, within the bound.
No kernel may reach another device: no remote copies, remote signals or barrier semaphores. Data moves between devices by JAX's collectives and lax.ppermute only.
A program may use at most 128 MiB of HBM per device.

v0:
```python
import math

import jax
import jax.numpy as jnp
from jax import lax
from jax.sharding import PartitionSpec as P

HEAD_DIM = 128


rope_theta = 1000000.0
neg_large = -1e30


def locate(global_rows, lengths):
    boundary = jnp.cumsum(lengths)
    segment_ids = jnp.sum((global_rows[:, None] >= boundary[None, :]).astype(jnp.int32), axis=1)
    starting = boundary - lengths
    member = segment_ids[:, None] == jnp.arange(lengths.shape[0], dtype=jnp.int32)[None, :]
    positions = global_rows - jnp.sum(jnp.where(member, starting[None, :], 0), axis=1)
    return (segment_ids, positions, member)


def rotary_tables(positions, head_dim):
    half_dim = head_dim // 2
    exponent = jnp.arange(half_dim, dtype=jnp.float32) * (2.0 / head_dim)
    inverse = jnp.exp(-math.log(rope_theta) * exponent)
    angles = positions.astype(jnp.float32)[:, None] * inverse[None, :]
    return (jnp.cos(angles), jnp.sin(angles))


def rotate(values, cosine_table, sine_table, direction):
    half_dim = values.shape[-1] // 2
    first_half = values[..., :half_dim]
    second_half = values[..., half_dim:]
    cosine_part = cosine_table[:, None, :]
    sine_part = sine_table[:, None, :] * direction
    return jnp.concatenate(
        [
            first_half * cosine_part - second_half * sine_part,
            second_half * cosine_part + first_half * sine_part,
        ],
        axis=-1,
    )


def attend_all(
    set_queries,
    set_grads,
    set_rows,
    set_segments,
    all_keys,
    all_values,
    all_segments,
    local_kv,
    head_dim,
):
    count_rows = set_queries.shape[0]
    total_tokens = all_keys.shape[0]
    group_size = set_queries.shape[1] // (local_kv * head_dim)
    score_scale = 1.0 / math.sqrt(head_dim)
    block_size = min(512, total_tokens)
    block_count = total_tokens // block_size
    query_heads = set_queries.reshape(count_rows, local_kv, group_size, head_dim)
    grad_heads = set_grads.reshape(count_rows, local_kv, group_size, head_dim)
    key_blocks = all_keys.reshape(block_count, block_size, local_kv, head_dim)
    value_blocks = all_values.reshape(block_count, block_size, local_kv, head_dim)
    segment_blocks = all_segments.reshape(block_count, block_size)
    block_starts = jnp.arange(block_count, dtype=jnp.int32) * block_size

    def allowed_mask(block_start, block_segments):
        key_rows = block_start + jnp.arange(block_size, dtype=jnp.int32)
        return (key_rows[None, :] <= set_rows[:, None]) & (
            block_segments[None, :] == set_segments[:, None]
        )

    def block_scores(key_block, allowed):
        scores = (
            jnp.einsum("tkgd,ukd->kgtu", query_heads, key_block, preferred_element_type=jnp.float32)
            * score_scale
        )
        return jnp.where(allowed[None, None], scores, neg_large)

    def first_pass(softmax_state, inputs):
        key_block, block_start, block_segments = inputs
        allowed = allowed_mask(block_start, block_segments)

        def first_update(current):
            running_max, running_sum = current
            scores = block_scores(key_block, allowed)
            new_max = jnp.maximum(running_max, jnp.max(scores, axis=-1))
            weights = jnp.where(allowed[None, None], jnp.exp(scores - new_max[..., None]), 0.0)
            return (
                new_max,
                running_sum * jnp.exp(running_max - new_max) + jnp.sum(weights, axis=-1),
            )

        return (
            lax.cond(jnp.any(allowed), first_update, lambda current: current, softmax_state),
            None,
        )

    start_max = jnp.full((local_kv, group_size, count_rows), neg_large, jnp.float32)
    start_sum = jnp.zeros((local_kv, group_size, count_rows), jnp.float32)
    (final_max, final_sum), _ = lax.scan(
        first_pass, (start_max, start_sum), (key_blocks, block_starts, segment_blocks)
    )
    log_total = final_max + jnp.log(final_sum)

    def second_pass(output_sum, inputs):
        key_block, value_block, block_start, block_segments = inputs
        allowed = allowed_mask(block_start, block_segments)

        def second_update(current):
            scores = block_scores(key_block, allowed)
            probabilities = jnp.where(
                allowed[None, None], jnp.exp(scores - log_total[..., None]), 0.0
            ).astype(jnp.bfloat16)
            return current + jnp.einsum(
                "kgtu,ukd->tkgd", probabilities, value_block, preferred_element_type=jnp.float32
            )

        return (
            lax.cond(jnp.any(allowed), second_update, lambda current: current, output_sum),
            None,
        )

    zero_heads = jnp.zeros((count_rows, local_kv, group_size, head_dim), jnp.float32)
    output_sum, _ = lax.scan(
        second_pass, zero_heads, (key_blocks, value_blocks, block_starts, segment_blocks)
    )
    attended_heads = output_sum.astype(jnp.bfloat16)
    row_delta = jnp.einsum(
        "tkgd,tkgd->kgt", attended_heads, grad_heads, preferred_element_type=jnp.float32
    )

    def third_pass(query_grad, inputs):
        key_block, value_block, block_start, block_segments = inputs
        allowed = allowed_mask(block_start, block_segments)

        def third_update(current):
            scores = block_scores(key_block, allowed)
            probabilities = jnp.where(
                allowed[None, None], jnp.exp(scores - log_total[..., None]), 0.0
            )
            rounded = probabilities.astype(jnp.bfloat16)
            prob_grad = jnp.einsum(
                "tkgd,ukd->kgtu", grad_heads, value_block, preferred_element_type=jnp.float32
            )
            score_grad = (probabilities * (prob_grad - row_delta[..., None])).astype(jnp.bfloat16)
            new_query = current + jnp.einsum(
                "kgtu,ukd->tkgd", score_grad, key_block, preferred_element_type=jnp.float32
            )
            key_part = jnp.einsum(
                "kgtu,tkgd->ukd", score_grad, query_heads, preferred_element_type=jnp.float32
            )
            value_part = jnp.einsum(
                "kgtu,tkgd->ukd", rounded, grad_heads, preferred_element_type=jnp.float32
            )
            return (new_query, key_part, value_part)

        def skipped(current):
            empty = jnp.zeros((block_size, local_kv, head_dim), jnp.float32)
            return (current, empty, empty)

        new_query, key_part, value_part = lax.cond(
            jnp.any(allowed), third_update, skipped, query_grad
        )
        return (new_query, (key_part, value_part))

    query_grad, (key_parts, value_parts) = lax.scan(
        third_pass, zero_heads, (key_blocks, value_blocks, block_starts, segment_blocks)
    )
    key_cols = local_kv * head_dim
    kv_terms = jnp.concatenate(
        [key_parts.reshape(total_tokens, key_cols), value_parts.reshape(total_tokens, key_cols)],
        axis=1,
    )
    return (
        attended_heads.reshape(count_rows, set_queries.shape[1]),
        query_grad * score_scale,
        kv_terms,
    )


def shards(hidden, w_query, w_key, w_value, out_grad, lengths, advantages):
    head_dim = HEAD_DIM
    local_tokens = hidden.shape[0]
    devices_dp = lax.axis_size("dp")
    dp_index = lax.axis_index("dp")
    query_cols = w_query.shape[1]
    key_cols = w_key.shape[1]
    local_kv = key_cols // head_dim
    local_heads = query_cols // head_dim
    total_tokens = local_tokens * devices_dp
    score_scale = 1.0 / math.sqrt(head_dim)
    own_rows = dp_index * local_tokens + jnp.arange(local_tokens, dtype=jnp.int32)
    own_segments, own_positions, own_member = locate(own_rows, lengths)
    own_cosine, own_sine = rotary_tables(own_positions, head_dim)
    full_query, full_key, full_value = (
        lax.all_gather(w_query, "dp", axis=0, tiled=True),
        lax.all_gather(w_key, "dp", axis=0, tiled=True),
        lax.all_gather(w_value, "dp", axis=0, tiled=True),
    )
    proj_query = jnp.dot(hidden, full_query, preferred_element_type=jnp.float32)
    proj_key = jnp.dot(hidden, full_key, preferred_element_type=jnp.float32)
    proj_value = jnp.dot(hidden, full_value, preferred_element_type=jnp.float32)
    queries = (
        rotate(proj_query.reshape(local_tokens, local_heads, head_dim), own_cosine, own_sine, 1.0)
        .astype(jnp.bfloat16)
        .reshape(local_tokens, query_cols)
    )
    keys_own = (
        rotate(proj_key.reshape(local_tokens, local_kv, head_dim), own_cosine, own_sine, 1.0)
        .astype(jnp.bfloat16)
        .reshape(local_tokens, key_cols)
    )
    values_own = proj_value.astype(jnp.bfloat16)
    token_adv = jnp.sum(jnp.where(own_member, advantages[None, :], 0.0), axis=1)
    token_grad = (out_grad.astype(jnp.float32) * token_adv[:, None]).astype(jnp.bfloat16)
    all_keys, all_values = (
        lax.all_gather(keys_own, "dp", axis=0, tiled=True),
        lax.all_gather(values_own, "dp", axis=0, tiled=True),
    )
    all_segments, _, _ = locate(jnp.arange(total_tokens, dtype=jnp.int32), lengths)
    own_set_segments, set_positions, _ = locate(own_rows, lengths)
    set_attended, set_query_rot, kv_terms = attend_all(
        queries,
        token_grad,
        own_rows,
        own_set_segments,
        all_keys,
        all_values,
        all_segments,
        local_kv,
        head_dim,
    )
    set_cosine, set_sine = rotary_tables(set_positions, head_dim)
    set_dquery = (
        rotate(
            set_query_rot.reshape(local_tokens, local_heads, head_dim), set_cosine, set_sine, -1.0
        )
        .astype(jnp.bfloat16)
        .reshape(local_tokens, query_cols)
    )
    summed_terms = lax.psum_scatter(kv_terms, "dp", scatter_dimension=0, tiled=True)
    key_rot = (summed_terms[:, :key_cols] * score_scale).reshape(local_tokens, local_kv, head_dim)
    key_grad = (
        rotate(key_rot, own_cosine, own_sine, -1.0)
        .astype(jnp.bfloat16)
        .reshape(local_tokens, key_cols)
    )
    value_grad = summed_terms[:, key_cols:].astype(jnp.bfloat16)
    grad_cat = jnp.concatenate([set_dquery, key_grad, value_grad], axis=1)
    weight_total = lax.psum_scatter(
        lax.dot_general(
            hidden, grad_cat, (((0,), (0,)), ((), ())), preferred_element_type=jnp.float32
        ).astype(jnp.bfloat16),
        "dp",
        scatter_dimension=0,
        tiled=True,
    )
    grad_w_query = weight_total[:, :query_cols]
    grad_w_key = weight_total[:, query_cols : query_cols + key_cols]
    grad_w_value = weight_total[:, query_cols + key_cols :]
    contract_cols = (((1,), (1,)), ((), ()))
    partial_hidden = lax.dot_general(
        set_dquery, full_query, contract_cols, preferred_element_type=jnp.float32
    )
    partial_hidden = partial_hidden + lax.dot_general(
        key_grad, full_key, contract_cols, preferred_element_type=jnp.float32
    )
    partial_hidden = partial_hidden + lax.dot_general(
        value_grad, full_value, contract_cols, preferred_element_type=jnp.float32
    )
    grad_hidden = lax.psum_scatter(
        partial_hidden.astype(jnp.bfloat16), "mp", scatter_dimension=1, tiled=True
    )
    return (set_attended, grad_hidden, grad_w_query, grad_w_key, grad_w_value)


def solution(mesh):
    return jax.shard_map(
        shards,
        mesh=mesh,
        in_specs=(
            P("dp", None),
            P("dp", "mp"),
            P("dp", "mp"),
            P("dp", "mp"),
            P("dp", "mp"),
            P(),
            P(),
        ),
        out_specs=(P("dp", "mp"), P("dp", "mp"), P("dp", "mp"), P("dp", "mp"), P("dp", "mp")),
        check_vma=False,
    )
```

profile of v0, /device:TPU:1, one launch (start us, length us, event | category | flops | bytes accessed | tf_op | source)
XLA Modules:
  0.0 1605.5 jit_solution(15517650427880605709)
XLA Ops:
  11.2 131.6 %all-gather.10.cloned.1.call-done = bf16[5120,128]{1,0:T(8,128)(2,1)} async-done(((bf16[160,128]{1,0:T(8,128)(2,1)}), bf16[5120,128]{1,0:T(8,128)(2,1)}) %all-gather.10.cloned.1.call-update) | async-done | bytes 1310736 | tf_op jit(solution)/shard_map/all_gather | solution.py:202
  142.8 2.0 convolution_bitcast_fusion.1
  148.9 147.4 %all-gather.6.cloned.1.call-done = bf16[5120,128]{1,0:T(8,128)(2,1)} async-done(((bf16[160,128]{1,0:T(8,128)(2,1)}), bf16[5120,128]{1,0:T(8,128)(2,1)}) %all-gather.6.cloned.1.call-update) | async-done | bytes 1310736 | tf_op jit(solution)/shard_map/all_gather | solution.py:203
  296.2 2.6 convolution_convert_fusion.1
  299.1 251.3 %all-gather.14.cloned.1.call-done = bf16[5120,1024]{1,0:T(8,128)(2,1)} async-done(((bf16[160,1024]{1,0:T(8,128)(2,1)}), bf16[5120,1024]{1,0:T(8,128)(2,1)}) %all-gather.14.cloned.1.call-update) | async-done | bytes 10485776 | tf_op jit(solution)/shard_map/all_gather | solution.py:201
  550.3 6.2 convolution_bitcast_fusion
  557.5 126.5 %all-gather.12.cloned.1.call-done = bf16[6144,128]{1,0:T(8,128)(2,1)} async-done(((bf16[192,128]{1,0:T(8,128)(2,1)}), bf16[6144,128]{1,0:T(8,128)(2,1)}) %all-gather.12.cloned.1.call-update) | async-done | bytes 1572880 | tf_op jit(solution)/shard_map/all_gather | solution.py:222
  684.0 39.7 %while.45 = (s32[]{:T(128)}, f32[1,8,192]{2,1,0:T(8,128)S(1)}, f32[1,8,192]{2,1,0:T(8,128)S(1)}, s32[12]{0:T(128)}, s32[12,512]{1,0:T(8,128)S(1)}, /*index=5*/s3...) while((s32[]{:T(128)}, f32[1,8,192]{2,1,0:T(8,128)S(1)}, ...), condition=%wide.region_10.11_spmd.clone, body=%wide.region_4.10_spmd.clone.sunk | while | flops 208015040 | bytes 7203811 | solution.py:105
  687.1 2.8 conditional.9
  687.1 1.6 fusion.6
  723.8 114.1 %all-gather.8.cloned.1.call-done = bf16[6144,128]{1,0:T(8,128)(2,1)} async-done(((bf16[192,128]{1,0:T(8,128)(2,1)}), bf16[6144,128]{1,0:T(8,128)(2,1)}) %all-gather.8.cloned.1.call-update) | async-done | bytes 1572880 | tf_op jit(solution)/shard_map/all_gather | solution.py:223
  838.8 43.3 %while.46 = (s32[]{:T(128)}, f32[192,1,8,128]{3,0,2,1:T(8,128)}, s32[12]{0:T(128)}, s32[12,512]{1,0:T(8,128)S(1)}, s32[192]{0:T(256)S(1)}, /*index=5*/bf16[12,51...) while((s32[]{:T(128)}, f32[192,1,8,128]{3,0,2,1:T(8,128)}, ...), condition=%wide.region_15.16_spmd.clone, body=%wide.region_11.15_spmd.clone.sunk | while | flops 407175872 | bytes 2444755 | solution.py:129
  838.8 1.2 dynamic_slice.104
  842.1 3.4 conditional.10
  842.1 3.4 fusion.21
  845.5 1.2 dynamic_slice.104
  848.9 1.2 dynamic_slice.104
  852.2 1.2 dynamic_slice.104
  855.5 1.2 dynamic_slice.104
  858.8 1.2 dynamic_slice.104
  862.2 1.2 dynamic_slice.104
  865.5 1.2 dynamic_slice.104
  868.8 1.2 dynamic_slice.104
  872.1 1.2 dynamic_slice.104
  875.5 1.2 dynamic_slice.104
  878.8 1.2 dynamic_slice.104
  882.1 2.0 bitcast_convert_fusion
  885.4 58.1 %while.47 = (s32[]{:T(128)}, f32[192,1,8,128]{3,0,2,1:T(8,128)S(1)}, f32[12,512,1,128]{3,1,2,0:T(8,128)}, f32[12,512,1,128]{3,1,2,0:T(8,128)}, s32[12]{0:T(128)}...) while((s32[]{:T(128)}, ...), condition=%wide.region_21.22_spmd.clone, body=%wide.region_17.21_spmd.clone.sunk | while | flops 1016660672 | bytes 21193292 | solution.py:171
  885.4 1.2 dynamic_slice.106
  888.7 7.5 conditional.11
  888.7 1.5 fusion.66
  890.3 2.3 fusion.38
  892.6 1.3 fusion.57
  893.9 1.6 fusion.54
  897.0 1.2 dynamic_slice.106
  909.7 1.2 dynamic_slice.106
  913.9 1.2 dynamic_slice.106
  918.1 1.2 dynamic_slice.106
  943.5 5.9 pad_maximum_fusion
  951.8 274.8 %reduce-scatter.6.cloned.1.call-done = f32[192,256]{1,0:T(8,128)} async-done(((f32[6144,256]{1,0:T(8,128)}), f32[192,256]{1,0:T(8,128)}) %reduce-scatter.6.cloned.1.call-update) | async-done | bytes 196624 | tf_op jit(solution)/shard_map/reduce_scatter | solution.py:246
  1228.9 6.7 fusion.80
  1235.6 17.7 %copy.69 = bf16[5120,1280]{1,0:T(8,128)(2,1)} copy(bf16[5120,1280]{0,1:T(8,128)(2,1)} %fusion.80) | data formatting | bytes 26214400
  1253.3 7.9 fusion.111
  1262.6 1.9 fusion.81
  1265.7 292.0 %reduce-scatter.10.cloned.1.call-done = bf16[160,1280]{1,0:T(8,128)(2,1)} async-done(((bf16[5120,1280]{1,0:T(8,128)(2,1)}), bf16[160,1280]{1,0:T(8,128)(2,1)}) %reduce-scatter.10.cloned.1.call-update) | async-done | bytes 409616
  1557.7 1.7 slice.63
  1559.4 1.4 fusion.116
  1560.8 37.9 %reduce-scatter.8.cloned.1.call-done = bf16[192,1280]{1,0:T(8,128)(2,1)} async-done(((bf16[192,5120]{1,0:T(8,128)(2,1)}), bf16[192,1280]{1,0:T(8,128)(2,1)}) %reduce-scatter.8.cloned.1.call-update) | async-done | bytes 491536 | tf_op jit(solution)/shard_map/reduce_scatter | solution.py:276
  (323 shorter events, 104.5 us)
Async XLA Ops:
  7.2 135.6 %copy-start = (bf16[192,5120]{1,0:T(8,128)(2,1)S(1)}, bf16[192,5120]{1,0:T(8,128)(2,1)}, u32[]{:S(2)}) copy-start(bf16[192,5120]{1,0:T(8,128)(2,1)} %param.19) | copy-start | bytes 5898244
  7.2 139.0 %copy-start.15 = (f32[4]{0:T(128)S(1)}, f32[4]{0:T(128)}, u32[]{:S(2)}) copy-start(f32[4]{0:T(128)} %param.25) | copy-start | bytes 52
  7.2 139.1 %copy-start.9 = (bf16[192,1024]{1,0:T(8,128)(2,1)S(1)}, bf16[192,1024]{1,0:T(8,128)(2,1)}, u32[]{:S(2)}) copy-start(bf16[192,1024]{1,0:T(8,128)(2,1)} %param.23) | copy-start | bytes 1179652
  7.2 135.6 %all-gather.10.cloned.1.call-start = ((), (), s32[]{:S(2)}) async-start(), calls=%async_computation.5 | async-start | bytes 1351680 | tf_op jit(solution)/shard_map/all_gather | solution.py:202
  7.9 288.3 %all-gather.6.cloned.1.call-start = ((), (), s32[]{:S(2)}) async-start(), calls=%async_computation.3 | async-start | bytes 1351680 | tf_op jit(solution)/shard_map/all_gather | solution.py:203
  8.7 541.7 %all-gather.14.cloned.1.call-start = ((), (), s32[]{:S(2)}) async-start(), calls=%async_computation.7 | async-start | bytes 10813440 | tf_op jit(solution)/shard_map/all_gather | solution.py:201
  9.4 674.6 %all-gather.12.cloned.1.call-start = ((), (), s32[]{:S(2)}) async-start(), calls=%async_computation.6 | async-start | bytes 1622016 | tf_op jit(solution)/shard_map/all_gather | solution.py:222
  10.3 137.5 %copy-start.13 = (f32[64]{0:T(128)}, f32[64]{0:T(128)S(1)}, u32[]{:S(2)}) copy-start(f32[64]{0:T(128)S(1)} %multiply_exponential_fusion) | copy-start | bytes 772
  145.9 691.9 %all-gather.8.cloned.1.call-start = ((), (), s32[]{:S(2)}) async-start(), calls=%async_computation.4 | async-start | bytes 1622016 | tf_op jit(solution)/shard_map/all_gather | solution.py:223
  148.9 408.1 %copy-start.6 = (f32[192,64]{1,0:T(8,128)}, f32[192,64]{1,0:T(8,128)S(1)}, u32[]{:S(2)}) copy-start(f32[192,64]{1,0:T(8,128)S(1)} %get-tuple-element.692) | copy-start | bytes 147460
  298.9 927.7 %reduce-scatter.6.cloned.1.call-start = ((), (), s32[]{:S(2)}) async-start(), calls=%async_computation.8 | async-start | bytes 6488064 | tf_op jit(solution)/shard_map/reduce_scatter | solution.py:246
  888.7 1.5 copy-start.10
  888.7 1.5 copy-start.12
  949.4 0.9 copy-start.7
  949.4 0.9 copy-start.8
  949.4 278.1 %copy-start.14 = (f32[64]{0:T(128)S(1)}, f32[64]{0:T(128)}, u32[]{:S(2)}) copy-start(f32[64]{0:T(128)} %copy-done.13) | copy-start | bytes 772
  949.4 608.2 %reduce-scatter.10.cloned.1.call-start = ((), (), s32[]{:S(2)}) async-start(), calls=%async_computation.10 | async-start | bytes 13516800
  950.7 0.7 copy-start.3
  950.7 0.9 copy-start.4
  1253.3 8.0 copy-start.1
  1253.3 345.4 %reduce-scatter.8.cloned.1.call-start = ((), (), s32[]{:S(2)}) async-start(), calls=%async_computation.9 | async-start | bytes 2457600 | tf_op jit(solution)/shard_map/reduce_scatter | solution.py:276
  1261.3 1.3 copy-start.2
  1261.3 1.3 copy-start.11
  1262.6 2.0 copy-start.5
Sparse Core Ops, SparseCore 0:
  9.7 133.0 all-gather.9
  144.4 151.7 all-gather.5
  297.9 252.4 all-gather.13
  552.4 131.5 all-gather.11
  685.5 152.2 all-gather.7
  949.5 276.9 reduce-scatter.5
  1253.4 304.2 reduce-scatter.9
  1561.1 37.5 reduce-scatter.7
where the time goes:
time: 1610 us
  waiting for transfers between devices  1380 us (86%)
  local copies, waits for them, and re-layouts  81.9 us (5%)
  other arithmetic  66.7 us (4%)
  matrix products  40.5 us (3%)
  loops' own time  23.6 us (1%)
    unnamed x9, waiting for transfers between devices  294 us
    reduce_scatter x1, waiting for transfers between devices, shards(): lax.psum_scatter(kv_terms, 'dp', scatter_dimension=0, tiled=True)  275 us
    all_gather x1, waiting for transfers between devices, shards(): lax.all_gather(w_query, 'dp', axis=0, tiled=True)  251 us
    all_gather x1, waiting for transfers between devices, shards(): lax.all_gather(w_value, 'dp', axis=0, tiled=True)  147 us
    all_gather x1, waiting for transfers between devices, shards(): lax.all_gather(w_key, 'dp', axis=0, tiled=True)  132 us
    all_gather x1, waiting for transfers between devices, shards(): lax.all_gather(keys_own, 'dp', axis=0, tiled=True)  127 us
    all_gather x1, waiting for transfers between devices, shards(): lax.all_gather(values_own, 'dp', axis=0, tiled=True)  114 us
    dynamic_slice x72, local copies, waits for them, and re-layouts, attend_all(): lax.scan(first_pass, (start_max, start_sum), (key_blocks, block_starts, s...  43.4 us
  transfers between devices with their start and end apart: 8, of which 8 were waited for; matrix products, arithmetic and copies ran while one was open for 4% of the time, Pallas kernels for 0%

commit v1 on v0

v1 whole, which is shorter than its diff:
```python
import math

import jax
import jax.numpy as jnp
from jax import lax
from jax.experimental import pallas as pl
from jax.experimental.pallas import tpu as pltpu
from jax.sharding import Mesh, PartitionSpec as P

HEAD_DIM = 128
HALF = 64
ROPE_THETA = 1000000.0
NEG_LARGE = -1e30
SCALE = 1.0 / math.sqrt(HEAD_DIM)
LOG2E = 1.4426950408889634
SIDE = 4
PLANE = SIDE * SIDE
BLOCK = 384
VMEM_LIMIT = 56 * 1024 * 1024


def fetch(value, axis, step):
    return lax.ppermute(value, axis, [(i, (i - step) % SIDE) for i in range(SIDE)])


def push(value, axis, step):
    return lax.ppermute(value, axis, [(i, (i + step) % SIDE) for i in range(SIDE)])


def plane_index(x, y, c):
    return (x * SIDE + y) * 2 + c


def cross_push(value, step, first):
    pairs = []
    for x in range(SIDE):
        for y in range(SIDE):
            for c in range(2):
                along_x = (c == 0) == first
                target = ((x + step) % SIDE, y) if along_x else (x, (y + step) % SIDE)
                pairs.append((plane_index(x, y, c), plane_index(*target, c)))
    return lax.ppermute(value, ("x", "y", "c"), pairs)


def swap_core(value):
    return lax.ppermute(value, "c", [(0, 1), (1, 0)])


ROUND = [(0, 1), (3, 2), (1, 3), (2, 0)]
ROUND_BACK = [(b, a) for a, b in ROUND]
CROSS = [(1, 2), (2, 1)]


def regroup(half0, half1, zl, c):
    first = jnp.where(zl == 0, half0, half1)
    second = jnp.where(zl == 0, half1, half0)
    moved = lax.ppermute(second, ("zl", "c"), ROUND)
    crossed = lax.ppermute(first, ("zl", "c"), CROSS)
    own = jnp.where(zl == c, first, moved)
    other = jnp.where(zl == c, moved, crossed)
    return own, other


def ungroup(own, other, zl, c):
    moved = lax.ppermute(jnp.where(zl == c, other, own), ("zl", "c"), ROUND_BACK)
    crossed = lax.ppermute(other, ("zl", "c"), CROSS)
    first = jnp.where(zl == c, own, crossed)
    half0 = jnp.where(zl == 0, first, moved)
    half1 = jnp.where(zl == 0, moved, first)
    return half0, half1


def in_order(own, other, zl):
    return jnp.where(zl == 0, own, other), jnp.where(zl == 0, other, own)


def gather_rows(rows0, rows1):
    strips = []
    for rows, near, far in ((rows0, "x", "y"), (rows1, "y", "x")):
        line = jnp.concatenate([rows] + [fetch(rows, near, s) for s in (1, 2, 3)], axis=0)
        strips += [line] + [fetch(line, far, s) for s in (1, 2, 3)]
    return jnp.concatenate(strips, axis=0)


def total(parts):
    result = parts[0].astype(jnp.float32)
    for part in parts[1:]:
        result = result + part.astype(jnp.float32)
    return result.astype(jnp.bfloat16)


def scatter_rows(terms):
    half = terms.shape[0] // 2
    results = []
    for start, near, far in ((0, "x", "y"), (half, "y", "x")):
        chunk = half // SIDE
        strips = [terms[start + s * chunk : start + (s + 1) * chunk] for s in range(SIDE)]
        line = total([strips[0]] + [push(strips[s], far, s) for s in (1, 2, 3)])
        small = chunk // SIDE
        pieces = [line[s * small : (s + 1) * small] for s in range(SIDE)]
        results.append(total([pieces[0]] + [push(pieces[s], near, s) for s in (1, 2, 3)]))
    return results


def permute_body(index_ref, source_ref, result_ref):
    @pl.loop(0, result_ref.shape[0])
    def _(i):
        result_ref[i] = source_ref[index_ref[i]]


def permute_blocks(source, index):
    vmem = pl.BlockSpec(memory_space=pltpu.VMEM)
    return pl.pallas_call(
        permute_body,
        out_shape=jax.ShapeDtypeStruct(source.shape, source.dtype),
        in_specs=[pl.BlockSpec(memory_space=pltpu.SMEM), vmem],
        out_specs=vmem,
        compiler_params=pltpu.CompilerParams(vmem_limit_bytes=VMEM_LIMIT),
        cost_estimate=pl.CostEstimate(
            flops=0, bytes_accessed=2 * source.size * source.dtype.itemsize, transcendentals=0
        ),
    )(index, source)


def attention_body(
    scalar_ref,
    key_slot_ref,
    value_slot_ref,
    token_ref,
    lowest_ref,
    query_t_ref,
    query_ref,
    grad_t_ref,
    grad_ref,
    key_ref,
    value_ref,
    attended_ref,
    dquery_ref,
    dkey_ref,
    dvalue_ref,
    probs_ref,
    tops_ref,
):
    first_block = scalar_ref[0]
    last_block = scalar_ref[1]
    mask_below = scalar_ref[2]
    rows = query_t_ref.shape[1]
    token = token_ref[...]
    lowest = lowest_ref[...]

    dkey_ref[...] = jnp.zeros_like(dkey_ref)
    dvalue_ref[...] = jnp.zeros_like(dvalue_ref)

    def forward(b, carry):
        top, weight, output = carry
        keys = key_ref[key_slot_ref[b]]
        scores = jnp.dot(keys, query_t_ref[...], preferred_element_type=jnp.float32)
        scores = scores * (SCALE * LOG2E)

        def masked(s):
            position = b * BLOCK + lax.broadcasted_iota(jnp.int32, s.shape, 0)
            return jnp.where((position <= token) & (position >= lowest), s, NEG_LARGE)

        scores = lax.cond((b == last_block) | (b <= mask_below), masked, lambda s: s, scores)
        new_top = jnp.maximum(top, jnp.max(scores, axis=0, keepdims=True))
        probs = jnp.exp2(scores - new_top)
        fade = jnp.exp2(top - new_top)
        rounded = probs.astype(jnp.bfloat16)
        probs_ref[b] = rounded
        tops_ref[b] = new_top
        weight = weight * fade + jnp.sum(probs, axis=0, keepdims=True)
        values_t = value_ref[value_slot_ref[b]].T
        output = output * fade + jnp.dot(values_t, rounded, preferred_element_type=jnp.float32)
        return new_top, weight, output

    top, weight, output = lax.fori_loop(
        first_block,
        last_block + 1,
        forward,
        (
            jnp.full((1, rows), NEG_LARGE, jnp.float32),
            jnp.zeros((1, rows), jnp.float32),
            jnp.zeros((HEAD_DIM, rows), jnp.float32),
        ),
    )
    inverse = 1.0 / weight
    attended = (output * inverse).astype(jnp.bfloat16)
    attended_ref[...] = attended
    delta = jnp.sum(
        attended.astype(jnp.float32) * grad_t_ref[...].astype(jnp.float32), axis=0, keepdims=True
    )

    def backward(b, dquery):
        key_slot = key_slot_ref[b]
        value_slot = value_slot_ref[b]
        prob_grad = jnp.dot(value_ref[value_slot], grad_t_ref[...], preferred_element_type=jnp.float32)
        probs = probs_ref[b].astype(jnp.float32) * (jnp.exp2(tops_ref[b] - top) * inverse)
        score_grad = (probs * (prob_grad - delta)).astype(jnp.bfloat16)
        dvalue_ref[value_slot] = jnp.dot(
            probs.astype(jnp.bfloat16), grad_ref[...], preferred_element_type=jnp.float32
        )
        dkey_ref[key_slot] = jnp.dot(score_grad, query_ref[...], preferred_element_type=jnp.float32)
        return dquery + jnp.dot(key_ref[key_slot].T, score_grad, preferred_element_type=jnp.float32)

    dquery = lax.fori_loop(
        first_block, last_block + 1, backward, jnp.zeros((HEAD_DIM, rows), jnp.float32)
    )
    dquery_ref[...] = dquery * SCALE


def attention(scalars, key_slots, value_slots, token, lowest, query_t, grad_t, keys, values):
    rows = query_t.shape[1]
    vmem = pl.BlockSpec(memory_space=pltpu.VMEM)
    smem = pl.BlockSpec(memory_space=pltpu.SMEM)
    kv = jax.ShapeDtypeStruct((PLANE, BLOCK, HEAD_DIM), jnp.float32)
    pairs = PLANE * BLOCK * rows // 2
    return pl.pallas_call(
        attention_body,
        out_shape=(
            jax.ShapeDtypeStruct((HEAD_DIM, rows), jnp.bfloat16),
            jax.ShapeDtypeStruct((HEAD_DIM, rows), jnp.float32),
            kv,
            kv,
        ),
        in_specs=[smem] * 3 + [vmem] * 8,
        out_specs=(vmem,) * 4,
        scratch_shapes=[
            pltpu.VMEM((PLANE, BLOCK, rows), jnp.bfloat16),
            pltpu.VMEM((PLANE, 1, rows), jnp.float32),
        ],
        compiler_params=pltpu.CompilerParams(vmem_limit_bytes=VMEM_LIMIT),
        cost_estimate=pl.CostEstimate(
            flops=pairs * HEAD_DIM * 12, bytes_accessed=16 * 1024 * 1024, transcendentals=pairs
        ),
    )(
        scalars,
        key_slots,
        value_slots,
        token,
        lowest,
        query_t,
        query_t.T,
        grad_t,
        grad_t.T,
        keys,
        values,
    )


def rotate_t(values, cosine, sine):
    parts = []
    for start in range(0, values.shape[0], HEAD_DIM):
        upper = values[start : start + HALF]
        lower = values[start + HALF : start + HEAD_DIM]
        parts += [upper * cosine - lower * sine, lower * cosine + upper * sine]
    return jnp.concatenate(parts, axis=0)


def shards(hidden, w_query, w_key, w_value, out_grad, lengths, advantages):
    x, y = lax.axis_index("x"), lax.axis_index("y")
    zl, zh, c = lax.axis_index("zl"), lax.axis_index("zh"), lax.axis_index("c")
    local_tokens, width = hidden.shape
    row_block = w_query.shape[0]
    half_cols = w_query.shape[1] // 2
    pair_cols = 2 * HEAD_DIM

    w_half0 = jnp.concatenate([w_key, w_query[:, :half_cols]], axis=1)
    w_half1 = jnp.concatenate([w_value, w_query[:, half_cols:]], axis=1)
    w_own, w_other = regroup(w_half0, w_half1, zl, c)
    w_rows0, w_rows1 = in_order(w_own, w_other, zl)
    first_cols = HEAD_DIM + pair_cols
    w_first = gather_rows(w_rows0[:, :first_cols], w_rows1[:, :first_cols])
    w_second = gather_rows(w_rows0[:, first_cols:], w_rows1[:, first_cols:])

    z_pairs = []
    for a in range(2):
        for b in range(2):
            for d in range(2):
                z_pairs.append((a * 4 + b * 2 + d, (1 - a) * 4 + (b ^ d) * 2 + d))
    hidden_other = lax.ppermute(hidden, ("zl", "zh", "c"), z_pairs)
    hidden_pair = jnp.concatenate(in_order(hidden, hidden_other, zl), axis=0)

    slot = jnp.arange(2 * PLANE, dtype=jnp.int32)
    inner = slot % PLANE
    slow, fast = inner // SIDE, inner % SIDE
    low = slot < PLANE
    dx, dy = jnp.where(low, fast, slow), jnp.where(low, slow, fast)
    relative = (((x + dx) % SIDE) * SIDE + (y + dy) % SIDE) * 2 + jnp.where(low, 0, 1)
    ax, ay, al = slot // 8, (slot // 2) % SIDE, slot % 2
    rx, ry = (ax - x) % SIDE, (ay - y) % SIDE
    absolute = jnp.where(al == 0, ry * SIDE + rx, PLANE + rx * SIDE + ry)
    hidden_t = permute_blocks(
        hidden_pair.T.reshape(2 * PLANE, row_block, 2 * local_tokens), relative
    ).reshape(width, 2 * local_tokens)
    hidden_rel = hidden_t.T

    block = x * SIDE + y
    tokens = block * BLOCK + jnp.arange(BLOCK, dtype=jnp.int32)
    boundary = jnp.cumsum(lengths)
    segment = jnp.sum((tokens[:, None] >= boundary[None, :]).astype(jnp.int32), axis=1)
    member = segment[:, None] == jnp.arange(lengths.shape[0], dtype=jnp.int32)[None, :]
    start = jnp.sum(jnp.where(member, (boundary - lengths)[None, :], 0), axis=1)
    exponent = jnp.arange(HALF, dtype=jnp.float32) * (2.0 / HEAD_DIM)
    inverse = jnp.exp(-math.log(ROPE_THETA) * exponent)
    angles = inverse[:, None] * (tokens - start).astype(jnp.float32)[None, :]
    cosine, sine = jnp.cos(angles), jnp.sin(angles)
    kv_cosine = jnp.where(c == 0, cosine, 1.0)
    kv_sine = jnp.where(c == 0, sine, 0.0)

    own_tokens = block * BLOCK + zl * local_tokens + jnp.arange(local_tokens, dtype=jnp.int32)
    own_segment = jnp.sum((own_tokens[:, None] >= boundary[None, :]).astype(jnp.int32), axis=1)
    own_member = own_segment[:, None] == jnp.arange(lengths.shape[0], dtype=jnp.int32)[None, :]
    own_advantage = jnp.sum(jnp.where(own_member, advantages[None, :], 0.0), axis=1)
    token_grad = (out_grad.astype(jnp.float32) * own_advantage[:, None]).astype(jnp.bfloat16)
    tg_own, tg_other = regroup(token_grad[:, :half_cols], token_grad[:, half_cols:], zl, c)
    grad_t = jnp.concatenate(in_order(tg_own, tg_other, zl), axis=0).T

    first_t = jnp.dot(hidden_rel, w_first, preferred_element_type=jnp.float32).T
    kv = rotate_t(first_t[:HEAD_DIM], kv_cosine, kv_sine).astype(jnp.bfloat16).T
    query_t0 = rotate_t(first_t[HEAD_DIM:], cosine, sine).astype(jnp.bfloat16)

    line = jnp.stack([kv] + [cross_push(kv, SIDE - s, True) for s in (1, 2, 3)])
    area = jnp.concatenate([line] + [cross_push(line, SIDE - s, False) for s in (1, 2, 3)], axis=0)
    area_other = swap_core(area)
    keys = jnp.where(c == 0, area, area_other)
    values = jnp.where(c == 0, area_other, area)

    second_t = jnp.dot(hidden_rel, w_second, preferred_element_type=jnp.float32).T
    query_t1 = rotate_t(second_t, cosine, sine).astype(jnp.bfloat16)

    blocks = jnp.arange(PLANE, dtype=jnp.int32)
    bx, by = (blocks // SIDE - x) % SIDE, (blocks % SIDE - y) % SIDE
    key_slots = by * SIDE + bx
    value_slots = bx * SIDE + by
    scalars = jnp.stack([start[0] // BLOCK, block, start[BLOCK - 1] // BLOCK]).astype(jnp.int32)
    token_row = jnp.concatenate([tokens, tokens])[None, :]
    lowest_row = jnp.concatenate([start, start])[None, :]

    outs = []
    for pair, query_t in enumerate((query_t0, query_t1)):
        wide = [query_t, grad_t[pair * pair_cols : (pair + 1) * pair_cols]]
        wide = [jnp.concatenate([w[:HEAD_DIM], w[HEAD_DIM:]], axis=1) for w in wide]
        outs.append(
            attention(
                scalars, key_slots, value_slots, token_row, lowest_row, wide[0], wide[1], keys, values
            )
        )
    attended = jnp.concatenate(
        [o[0][:, h * BLOCK : (h + 1) * BLOCK] for o in outs for h in range(2)], axis=0
    ).T
    at0, at1 = attended[:local_tokens], attended[local_tokens:]
    at_halves = ungroup(*in_order(at0, at1, zl), zl, c)
    attended_out = jnp.concatenate(at_halves, axis=1)

    dquery_t = [
        rotate_t(
            jnp.concatenate([o[1][:, :BLOCK], o[1][:, BLOCK:]], axis=0), cosine, -sine
        ).astype(jnp.bfloat16)
        for o in outs
    ]

    dkey = (outs[0][2] + outs[1][2]).astype(jnp.bfloat16)
    dvalue = (outs[0][3] + outs[1][3]).astype(jnp.bfloat16)
    kept = jnp.where(c == 0, dkey, dvalue)
    area = total([kept, swap_core(jnp.where(c == 0, dvalue, dkey))])
    lines = area.reshape(SIDE, SIDE, BLOCK, HEAD_DIM)
    line = total([lines[0]] + [cross_push(lines[s], s, False) for s in (1, 2, 3)])
    dkv = line[0].astype(jnp.float32)
    for s in (1, 2, 3):
        dkv = dkv + cross_push(line[s], s, True).astype(jnp.float32)
    dkv_t = dkv.T * jnp.where(c == 0, SCALE, 1.0)
    dkv_t = rotate_t(dkv_t, kv_cosine, -kv_sine).astype(jnp.bfloat16)

    grad_first = jnp.concatenate([dkv_t, dquery_t[0]], axis=0).T
    grad_second = dquery_t[1].T
    dw = []
    for grad in (grad_second, grad_first):
        term = jnp.dot(hidden_t, grad, preferred_element_type=jnp.float32).astype(jnp.bfloat16)
        dw.append(scatter_rows(term))
    dw_rows = [jnp.concatenate([dw[1][i], dw[0][i]], axis=1) for i in range(2)]
    dw0, dw1 = ungroup(*in_order(dw_rows[0], dw_rows[1], zl), zl, c)
    grad_w_key = dw0[:, :HEAD_DIM]
    grad_w_value = dw1[:, :HEAD_DIM]
    grad_w_query = jnp.concatenate([dw0[:, HEAD_DIM:], dw1[:, HEAD_DIM:]], axis=1)

    w_all = jnp.concatenate([w_first, w_second], axis=1)
    w_all = permute_blocks(w_all.reshape(2 * PLANE, row_block, w_all.shape[1]), absolute)
    w_all = w_all.reshape(width, w_all.shape[-1])
    grad_all = jnp.concatenate([grad_first, grad_second], axis=1)
    dhidden = lax.dot_general(
        grad_all, w_all, (((1,), (1,)), ((), ())), preferred_element_type=jnp.float32
    ).astype(jnp.bfloat16)
    out_cols = width // 4
    tiles = [
        [
            [
                dhidden[a * local_tokens : (a + 1) * local_tokens, (2 * b + d) * out_cols : (2 * b + d + 1) * out_cols]
                for d in range(2)
            ]
            for b in range(2)
        ]
        for a in range(2)
    ]
    stacked = [jnp.stack([tiles[z % 2][z // 2][d] for z in range(4)]) for d in range(2)]
    keep = jnp.where(c == 0, stacked[0], stacked[1])
    give = jnp.where(c == 0, stacked[1], stacked[0])
    chip = total([keep, swap_core(give)])
    z = zh * 2 + zl
    ring = [(0, 0), (1, 0), (0, 1), (1, 1)]
    parts = [lax.dynamic_index_in_dim(chip, z, 0, keepdims=False)]
    for s in (1, 2, 3):
        pairs = [
            (ring[i][0] * 2 + ring[i][1], ring[(i + s) % 4][0] * 2 + ring[(i + s) % 4][1])
            for i in range(4)
        ]
        piece = lax.dynamic_index_in_dim(chip, (z + s) % 4, 0, keepdims=False)
        parts.append(lax.ppermute(piece, ("zl", "zh"), pairs))
    grad_hidden = total(parts)

    return attended_out, grad_hidden, grad_w_query, grad_w_key, grad_w_value


def solution(mesh):
    fine = Mesh(mesh.devices.reshape(SIDE, SIDE, 2, 2, 2), ("x", "y", "zl", "zh", "c"))
    dp, mp = ("x", "y", "zl"), ("zh", "c")
    return jax.shard_map(
        shards,
        mesh=fine,
        in_specs=(P(dp, None), P(dp, mp), P(dp, mp), P(dp, mp), P(dp, mp), P(), P()),
        out_specs=(P(dp, mp),) * 5,
        check_vma=False,
    )
```

time: 1610 us -> 460 us (0.29)
  waiting for transfers between devices: 1380 us -> 140 us
  starting transfers between devices: 0.72 us -> 179 us
  local copies, waits for them, and re-layouts: 81.9 us -> 36.3 us
  Pallas kernels: 0 us -> 27 us
  loops' own time: 23.6 us -> 0 us
  matrix products: 40.5 us -> 18.7 us
  other arithmetic: 66.7 us -> 45.6 us
    all_gather x5 -> x0, waiting for transfers between devices: 771 us -> none  [the longest x1 251 us: shards(): lax.all_gather(w_query, 'dp', axis=0, tiled=True)]
    reduce_scatter x2 -> x0, waiting for transfers between devices: 313 us -> none  [the longest x1 275 us: shards(): lax.psum_scatter(kv_terms, 'dp', scatter_dimension=0, tiled=True)]
    unnamed x9 -> x0, waiting for transfers between devices: 294 us -> none
    ppermute x0 -> x75, starting transfers between devices: none -> 179 us  [the longest x12 79.4 us: cross_push(): return lax.ppermute(value, ('x', 'y', 'c'), pairs)]
    ppermute x0 -> x75, waiting for transfers between devices: none -> 140 us  [the longest x24 56.7 us: fetch(): lax.ppermute(value, axis, [(i, (i - step) % SIDE) for i in range(SIDE)])]
    dynamic_slice x72 -> x0, local copies, waits for them, and re-layouts: 43.4 us -> none  [attend_all(): lax.scan(first_pass, (start_max, start_sum), (key_blocks, block_starts, s...]
    reduce_or x36 -> x0, other arithmetic: 28.4 us -> none  [the longest x12 9.69 us: third_pass(): jnp.any(allowed)]
    pallas_call x0 -> x4, Pallas kernels: none -> 27 us  [the longest x2 16 us: attention(): pl.pallas_call(attention_body, out_shape=(jax.ShapeDtypeStruct((HEAD_DIM,...]
  transfers between devices with their start and end apart: 8 -> 75, of which waited for: 8 -> 36; matrix products, arithmetic and copies ran while one was open for 4% -> 16% of each run, Pallas kernels for 0% -> 2%
where the time goes in v1:
time: 460 us; the launch traced here: 453 us
  starting transfers between devices  179 us (39%)
  waiting for transfers between devices  140 us (30%)
  other arithmetic  45.6 us (10%)
  local copies, waits for them, and re-layouts  36.3 us (8%)
  Pallas kernels  27 us (6%)
  matrix products  18.7 us (4%)
  between operations  5.83 us (1%)
    ppermute x12, starting transfers between devices, cross_push(): return lax.ppermute(value, ('x', 'y', 'c'), pairs)  79.4 us
    ppermute x24, waiting for transfers between devices, fetch(): lax.ppermute(value, axis, [(i, (i - step) % SIDE) for i in range(SIDE)])  56.7 us
    ppermute x24, waiting for transfers between devices, push(): lax.ppermute(value, axis, [(i, (i + step) % SIDE) for i in range(SIDE)])  30.6 us
    ppermute x24, starting transfers between devices, push(): lax.ppermute(value, axis, [(i, (i + step) % SIDE) for i in range(SIDE)])  29.6 us
    ppermute x24, starting transfers between devices, fetch(): lax.ppermute(value, axis, [(i, (i - step) % SIDE) for i in range(SIDE)])  28.6 us
    ppermute x12, waiting for transfers between devices, cross_push(): return lax.ppermute(value, ('x', 'y', 'c'), pairs)  22 us
    ppermute x3, starting transfers between devices, swap_core(): return lax.ppermute(value, 'c', [(0, 1), (1, 0)])  19.1 us
    ppermute x3, waiting for transfers between devices, shards(): parts.append(lax.ppermute(piece, ('zl', 'zh'), pairs))  17.2 us
  transfers between devices with their start and end apart: 75, of which 36 were waited for; matrix products, arithmetic and copies ran while one was open for 16% of the time, Pallas kernels for 2%

profile of v1, /device:TPU:1, one launch (start us, length us, event | category | flops | bytes accessed | tf_op | source)
XLA Modules:
  0.0 452.5 jit_solution(10064053629002623955)
XLA Ops:
  2.6 4.9 %collective-permute-start.1 = (bf16[160,640]{1,0:T(8,128)(2,1)S(1)}, bf16[160,640]{1,0:T(8,128)(2,1)S(1)}, u32[]{:S(2)}, u32[]{:S(2)}) collective-permute-start(bf16[160,640]{1,0:T(8,128)(2,1)S(1)} %get-tuple-element.85), channel_id=1, source_target_pairs={{1,4},{4,1},{3,6},{6,3},{9,12},{12,9},{11,14},{14,11},{17,20},{20,... | collective-permute-start | bytes 614408 | tf_op jit(solution)/shard_map/ppermute | solution.py:58
  22.4 13.9 %collective-permute-done.16 = bf16[192,512]{1,0:T(8,128)(2,1)S(1)} collective-permute-done((bf16[192,512]{1,0:T(8,128)(2,1)S(1)}, bf16[192,512]{1,0:T(8,128)(2,1)S(1)}, u32[]{:S(2)}, u32[]{:S(2)}) %collective-permute-start.16) | collective-permute-done | bytes 196640 | tf_op jit(solution)/shard_map/ppermute | solution.py:58
  37.2 2.5 collective-permute-start.24
  45.5 2.8 collective-permute-start.27
  51.4 2.8 collective-permute-start.5
  57.4 7.4 %collective-permute-done.5 = bf16[640,384]{1,0:T(8,128)(2,1)S(1)} collective-permute-done((bf16[640,384]{1,0:T(8,128)(2,1)S(1)}, bf16[640,384]{1,0:T(8,128)(2,1)S(1)}, u32[]{:S(2)}, u32[]{:S(2)}) %collective-permute-start.5) | collective-permute-done | bytes 491552 | tf_op jit(solution)/shard_map/ppermute | solution.py:23
  65.0 17.9 %collective-permute-done.7 = bf16[640,384]{1,0:T(8,128)(2,1)S(1)} collective-permute-done((bf16[640,384]{1,0:T(8,128)(2,1)S(1)}, bf16[640,384]{1,0:T(8,128)(2,1)S(1)}, u32[]{:S(2)}, u32[]{:S(2)}) %collective-permute-start.7) | collective-permute-done | bytes 491552 | tf_op jit(solution)/shard_map/ppermute | solution.py:23
  83.1 2.7 collective-permute-start.8
  88.3 2.6 collective-permute-done.10
  94.9 5.4 %collective-permute-done.11 = bf16[640,384]{1,0:T(8,128)(2,1)S(1)} collective-permute-done((bf16[640,384]{1,0:T(8,128)(2,1)S(1)}, bf16[640,384]{1,0:T(8,128)(2,1)S(1)}, u32[]{:S(2)}, u32[]{:S(2)}) %collective-permute-start.11) | collective-permute-done | bytes 491552 | tf_op jit(solution)/shard_map/ppermute | solution.py:23
  100.3 6.7 %collective-permute-start.31 = (bf16[160,256]{1,0:T(8,128)(2,1)}, bf16[160,256]{1,0:T(8,128)(2,1)}, u32[]{:S(2)}, u32[]{:S(2)}) collective-permute-start(bf16[160,256]{1,0:T(8,128)(2,1)} %get-tuple-element.119), channel_id=1, source_target_pairs={{0,16},{8,24},{16,0},{24,8},{1,17},{9,25},{17,1},{25,9},{2,18},{10... | collective-permute-start | bytes 245768 | tf_op jit(solution)/shard_map/ppermute | solution.py:23
  114.8 6.3 %copy.39 = bf16[5120,384]{1,0:T(8,128)(2,1)} copy(bf16[5120,384]{0,1:T(8,128)(2,1)} %maximum_bitcast_fusion) | data formatting | bytes 7864320 | tf_op jit(solution)/shard_map/transpose | solution.py:293
  121.1 4.7 %shard_map.110 = bf16[32,160,384]{2,1,0:T(8,128)(2,1)} custom-call(s32[32]{0:T(128)} %get-tuple-element.144.index_ref, bf16[32,160,384]{2,1,0:T(8,128)(2,1)} %bitcast.94), custom_call_target="tpu_custom_call" | custom-call | bytes 7864320 | tf_op jit(solution)/shard_map/pallas_call | solution.py:113
  125.9 4.3 fusion.136
  133.2 10.3 %collective-permute-start.18 = (bf16[384,128]{1,0:T(8,128)(2,1)S(1)}, bf16[384,128]{1,0:T(8,128)(2,1)S(1)}, u32[]{:S(2)}, u32[]{:S(2)}) collective-permute-start(bf16[384,128]{1,0:T(8,128)(2,1)S(1)} %fusion.95), channel_id=1, source_target_pairs={{0,64},{1,17},{8,72},{9,25},{16,80},{17,1},{24,88},{25,9},{32,96},... | collective-permute-start | bytes 294920 | tf_op jit(solution)/shard_map/ppermute | solution.py:42
  145.5 3.0 collective-permute-done.19
  152.0 3.5 collective-permute-done.20
  157.7 3.3 collective-permute-done.22
  161.8 12.5 %collective-permute-start.23 = (bf16[16,384,128]{2,1,0:T(8,128)(2,1)}, bf16[16,384,128]{2,1,0:T(8,128)(2,1)}, u32[]{:S(2)}, u32[]{:S(2)}) collective-permute-start(bf16[16,384,128]{2,1,0:T(8,128)(2,1)} %constant_dynamic-update-slice_fusion.14), channel_id=1, source_target_pairs={{0,1},{1,0},{2,3},{3,2},{4,5},{5,4},{6,7},{7,6},{8,9},{9,8},{10,11... | collective-permute-start | bytes 4718600 | tf_op jit(solution)/shard_map/ppermute | solution.py:46
  182.1 5.2 %collective-permute-done.33 = bf16[640,256]{1,0:T(8,128)(2,1)S(1)} collective-permute-done((bf16[640,256]{1,0:T(8,128)(2,1)S(1)}, bf16[640,256]{1,0:T(8,128)(2,1)S(1)}, u32[]{:S(2)}, u32[]{:S(2)}) %collective-permute-start.33) | collective-permute-done | bytes 327712 | tf_op jit(solution)/shard_map/ppermute | solution.py:23
  188.9 7.3 %collective-permute-done.35 = bf16[640,256]{1,0:T(8,128)(2,1)S(1)} collective-permute-done((bf16[640,256]{1,0:T(8,128)(2,1)S(1)}, bf16[640,256]{1,0:T(8,128)(2,1)S(1)}, u32[]{:S(2)}, u32[]{:S(2)}) %collective-permute-start.35) | collective-permute-done | bytes 327712 | tf_op jit(solution)/shard_map/ppermute | solution.py:23
  198.3 3.7 fusion.137
  202.1 3.8 broadcast_select_fusion.4
  206.0 8.1 %shard_map.111 = (bf16[128,768]{1,0:T(8,128)(2,1)}, f32[128,768]{1,0:T(8,128)}, f32[16,384,128]{2,1,0:T(8,128)}, f32[16,384,128]{2,1,0:T(8,128)}) custom-call(s32[3]{0:T(128)} %pad_add_fusion.2.scalar_ref, s32[16]{0:T(128)} %get-tuple-element.146.key_slot_ref, s32[16]{0:T(128)} %get-tuple-element.145.value_slot_ref, s32[1,768]{1,0:T(1,128)} %broadcast_in_dim.56.token_ref, ...), custom_call_target="tpu_custom_call" | custom-call | flops 3623878656 | bytes 16777216 | tf_op jit(solution)/shard_map/pallas_call | solution.py:217
  218.7 8.0 %shard_map.112 = (bf16[128,768]{1,0:T(8,128)(2,1)}, f32[128,768]{1,0:T(8,128)}, f32[16,384,128]{2,1,0:T(8,128)}, f32[16,384,128]{2,1,0:T(8,128)}) custom-call(s32[3]{0:T(128)} %pad_add_fusion.2.scalar_ref, s32[16]{0:T(128)} %get-tuple-element.146.key_slot_ref, s32[16]{0:T(128)} %get-tuple-element.145.value_slot_ref, s32[1,768]{1,0:T(1,128)} %broadcast_in_dim.56.token_ref, ...), custom_call_target="tpu_custom_call" | custom-call | flops 3623878656 | bytes 16777216 | tf_op jit(solution)/shard_map/pallas_call | solution.py:217
  226.7 6.2 %broadcast_select_fusion.3 = (bf16[16,384,128]{2,1,0:T(8,128)(2,1)}, bf16[16,384,128]{2,1,0:T(8,128)(2,1)S(1)}, bf16[16,384,128]{2,1,0:T(8,128)(2,1)S(1)}) fusion(pred[]{:T(512)S(6)} %eq.44, f32[16,384,128]{2,1,0:T(8,128)S(1)} %copy-done.4, f32[16,384,128]{2,1,0:T(8,128)} %get-tuple-element.16, f32[16,384,128]{2,1,0:T(8,128)} %get-tuple-element.17, ...), kind=kLoop, calls=%fused_computation.14 | loop fusion | flops 3932160 | bytes 17301504 | tf_op jit(solution)/shard_map/jit(_where)/select_n | solution.py:365
  233.4 6.4 %pad_maximum_fusion = bf16[5120,640]{1,0:T(8,128)(2,1)} fusion(bf16[5120,256]{1,0:T(8,128)(2,1)} %copy-done.5, bf16[5120,384]{1,0:T(8,128)(2,1)} %copy-done.2), kind=kLoop, calls=%fused_computation.2 | loop fusion | flops 13107200 | bytes 13107200 | tf_op jit(solution)/shard_map/concatenate | solution.py:386
  239.7 6.2 %shard_map.113 = bf16[32,160,640]{2,1,0:T(8,128)(2,1)} custom-call(s32[32]{0:T(128)} %get-tuple-element.143.index_ref, bf16[32,160,640]{2,1,0:T(8,128)(2,1)} %bitcast.93), custom_call_target="tpu_custom_call" | custom-call | bytes 13107200 | tf_op jit(solution)/shard_map/pallas_call | solution.py:113
  252.8 14.5 %collective-permute-start.39 = (bf16[4,384,128]{2,1,0:T(8,128)(2,1)S(1)}, bf16[4,384,128]{2,1,0:T(8,128)(2,1)S(1)}, u32[]{:S(2)}, u32[]{:S(2)}) collective-permute-start(bf16[4,384,128]{2,1,0:T(8,128)(2,1)S(1)} %get-tuple-element.61), channel_id=1, source_target_pairs={{0,8},{1,33},{8,16},{9,41},{16,24},{17,49},{24,0},{25,57},{32,40},... | collective-permute-start | bytes 1179656 | tf_op jit(solution)/shard_map/ppermute | solution.py:42
  267.4 32.7 %collective-permute-start.40 = (bf16[4,384,128]{2,1,0:T(8,128)(2,1)S(1)}, bf16[4,384,128]{2,1,0:T(8,128)(2,1)S(1)}, u32[]{:S(2)}, u32[]{:S(2)}) collective-permute-start(bf16[4,384,128]{2,1,0:T(8,128)(2,1)S(1)} %get-tuple-element.63), channel_id=1, source_target_pairs={{0,16},{1,65},{8,24},{9,73},{16,0},{17,81},{24,8},{25,89},{32,48},... | collective-permute-start | bytes 1179656 | tf_op jit(solution)/shard_map/ppermute | solution.py:42
  300.1 3.9 collective-permute-done.39
  304.1 5.4 %collective-permute-done.40 = bf16[4,384,128]{2,1,0:T(8,128)(2,1)S(1)} collective-permute-done((bf16[4,384,128]{2,1,0:T(8,128)(2,1)S(1)}, bf16[4,384,128]{2,1,0:T(8,128)(2,1)S(1)}, u32[]{:S(2)}, u32[]{:S(2)}) %collective-permute-start.40) | collective-permute-done | bytes 393248 | tf_op jit(solution)/shard_map/ppermute | solution.py:42
  312.0 13.1 %collective-permute-start.43 = (bf16[384,128]{1,0:T(8,128)(2,1)S(1)}, bf16[384,128]{1,0:T(8,128)(2,1)S(1)}, u32[]{:S(2)}, u32[]{:S(2)}) collective-permute-start(bf16[384,128]{1,0:T(8,128)(2,1)S(1)} %get-tuple-element.100), channel_id=1, source_target_pairs={{0,64},{1,17},{8,72},{9,25},{16,80},{17,1},{24,88},{25,9},{32,96},... | collective-permute-start | bytes 294920 | tf_op jit(solution)/shard_map/ppermute | solution.py:42
  335.2 3.6 collective-permute-start.56
  338.9 3.4 collective-permute-start.68
  343.5 6.2 %convolution_convert_fusion.1 = bf16[384,5120]{1,0:T(8,128)(2,1)S(1)} fusion(bf16[5120,640]{1,0:T(8,128)(2,1)} %bitcast.95, bf16[384,256]{1,0:T(8,128)(2,1)} %fusion.116, bf16[384,384]{1,0:T(8,128)(2,1)S(1)} %bitcast.96), kind=kOutput, calls=%fused_computation.1 | convolution fusion | flops 2519531520 | bytes 10977280 | tf_op jit(solution)/shard_map/dot_general | solution.py:390
  352.0 2.7 convolution_convert_fusion
  361.5 3.0 collective-permute-done.58
  369.7 6.9 %collective-permute-done.70 = bf16[160,256]{1,0:T(8,128)(2,1)S(1)} collective-permute-done((bf16[160,256]{1,0:T(8,128)(2,1)S(1)}, bf16[160,256]{1,0:T(8,128)(2,1)S(1)}, u32[]{:S(2)}, u32[]{:S(2)}) %collective-permute-start.70) | collective-permute-done | bytes 81952 | tf_op jit(solution)/shard_map/ppermute | solution.py:27
  378.4 2.7 collective-permute-start.63
  381.1 6.2 %collective-permute-start.45 = (bf16[4,192,1280]{2,1,0:T(8,128)(2,1)S(1)}, bf16[4,192,1280]{2,1,0:T(8,128)(2,1)S(1)}, u32[]{:S(2)}, u32[]{:S(2)}) collective-permute-start(bf16[4,192,1280]{2,1,0:T(8,128)(2,1)S(1)} %broadcast_select_fusion), channel_id=1, source_target_pairs={{0,1},{1,0},{2,3},{3,2},{4,5},{5,4},{6,7},{7,6},{8,9},{9,8},{10,11... | collective-permute-start | bytes 5898248 | tf_op jit(solution)/shard_map/ppermute | solution.py:46
  389.4 11.6 %collective-permute-done.61 = bf16[640,384]{1,0:T(8,128)(2,1)S(1)} collective-permute-done((bf16[640,384]{1,0:T(8,128)(2,1)S(1)}, bf16[640,384]{1,0:T(8,128)(2,1)S(1)}, u32[]{:S(2)}, u32[]{:S(2)}) %collective-permute-start.61) | collective-permute-done | bytes 491552 | tf_op jit(solution)/shard_map/ppermute | solution.py:27
  402.6 4.1 collective-permute-start.53
  407.8 3.0 collective-permute-done.53
  410.9 5.8 %collective-permute-start.65 = (bf16[160,384]{1,0:T(8,128)(2,1)S(1)}, bf16[160,384]{1,0:T(8,128)(2,1)S(1)}, u32[]{:S(2)}, u32[]{:S(2)}) collective-permute-start(bf16[160,384]{1,0:T(8,128)(2,1)S(1)} %get-tuple-element.83), channel_id=1, source_target_pairs={{0,16},{8,24},{16,0},{24,8},{1,17},{9,25},{17,1},{25,9},{2,18},{10... | collective-permute-start | bytes 368648 | tf_op jit(solution)/shard_map/ppermute | solution.py:27
  425.4 3.4 collective-permute-start.47
  433.8 4.9 %collective-permute-done.46 = bf16[192,1280]{1,0:T(8,128)(2,1)S(1)} collective-permute-done((bf16[192,1280]{1,0:T(8,128)(2,1)S(1)}, bf16[192,1280]{1,0:T(8,128)(2,1)S(1)}, u32[]{:S(2)}, u32[]{:S(2)}) %collective-permute-start.46) | collective-permute-done | bytes 491552 | tf_op jit(solution)/shard_map/ppermute | solution.py:417
  438.7 12.3 %collective-permute-done.47 = bf16[192,1280]{1,0:T(8,128)(2,1)S(1)} collective-permute-done((bf16[192,1280]{1,0:T(8,128)(2,1)S(1)}, bf16[192,1280]{1,0:T(8,128)(2,1)S(1)}, u32[]{:S(2)}, u32[]{:S(2)}) %collective-permute-start.47) | collective-permute-done | bytes 491552 | tf_op jit(solution)/shard_map/ppermute | solution.py:417
  (269 shorter events, 124.7 us)
Async XLA Ops:
  2.6 34.6 %collective-permute-start.1 = (bf16[160,640]{1,0:T(8,128)(2,1)S(1)}, bf16[160,640]{1,0:T(8,128)(2,1)S(1)}, u32[]{:S(2)}, u32[]{:S(2)}) collective-permute-start(bf16[160,640]{1,0:T(8,128)(2,1)S(1)} %get-tuple-element.85), channel_id=1, source_target_pairs={{1,4},{4,1},{3,6},{6,3},{9,12},{12,9},{11,14},{14,11},{17,20},{20,... | collective-permute-start | bytes 614408 | tf_op jit(solution)/shard_map/ppermute | solution.py:58
  7.5 29.6 %collective-permute-start = (bf16[160,640]{1,0:T(8,128)(2,1)S(1)}, bf16[160,640]{1,0:T(8,128)(2,1)S(1)}, u32[]{:S(2)}, u32[]{:S(2)}) collective-permute-start(bf16[160,640]{1,0:T(8,128)(2,1)S(1)} %get-tuple-element.84), channel_id=1, source_target_pairs={{0,1},{5,4},{1,5},{4,0},{2,3},{7,6},{3,7},{6,2},{8,9},{13,12},{9,1... | collective-permute-start | bytes 614408 | tf_op jit(solution)/shard_map/ppermute | solution.py:57
  7.6 102.9 %collective-permute-start.14 = (bf16[192,5120]{1,0:T(8,128)(2,1)}, bf16[192,5120]{1,0:T(8,128)(2,1)}, u32[]{:S(2)}, u32[]{:S(2)}) collective-permute-start(bf16[192,5120]{1,0:T(8,128)(2,1)} %param.7), channel_id=1, source_target_pairs={{0,4},{1,7},{2,6},{3,5},{4,0},{5,3},{6,2},{7,1},{8,12},{9,15},{10,... | collective-permute-start | bytes 5898248 | tf_op jit(solution)/shard_map/ppermute | solution.py:280
  12.7 23.6 %collective-permute-start.16 = (bf16[192,512]{1,0:T(8,128)(2,1)S(1)}, bf16[192,512]{1,0:T(8,128)(2,1)S(1)}, u32[]{:S(2)}, u32[]{:S(2)}) collective-permute-start(bf16[192,512]{1,0:T(8,128)(2,1)S(1)} %get-tuple-element.106), channel_id=1, source_target_pairs={{1,4},{4,1},{3,6},{6,3},{9,12},{12,9},{11,14},{14,11},{17,20},{20,... | collective-permute-start | bytes 589832 | tf_op jit(solution)/shard_map/ppermute | solution.py:58
  14.6 21.7 %collective-permute-start.15 = (bf16[192,512]{1,0:T(8,128)(2,1)S(1)}, bf16[192,512]{1,0:T(8,128)(2,1)S(1)}, u32[]{:S(2)}, u32[]{:S(2)}) collective-permute-start(bf16[192,512]{1,0:T(8,128)(2,1)S(1)} %get-tuple-element.105), channel_id=1, source_target_pairs={{0,1},{5,4},{1,5},{4,0},{2,3},{7,6},{3,7},{6,2},{8,9},{13,12},{9,1... | collective-permute-start | bytes 589832 | tf_op jit(solution)/shard_map/ppermute | solution.py:57
  45.5 9.9 %collective-permute-start.27 = (bf16[640,256]{1,0:T(8,128)(2,1)S(1)}, bf16[640,256]{1,0:T(8,128)(2,1)S(1)}, u32[]{:S(2)}, u32[]{:S(2)}) collective-permute-start(bf16[640,256]{1,0:T(8,128)(2,1)S(1)} %pad_maximum_fusion.7), channel_id=1, source_target_pairs={{0,24},{8,0},{16,8},{24,16},{1,25},{9,1},{17,9},{25,17},{2,26},{10... | collective-permute-start | bytes 983048 | tf_op jit(solution)/shard_map/ppermute | solution.py:23
  51.4 13.4 %collective-permute-start.5 = (bf16[640,384]{1,0:T(8,128)(2,1)S(1)}, bf16[640,384]{1,0:T(8,128)(2,1)S(1)}, u32[]{:S(2)}, u32[]{:S(2)}) collective-permute-start(bf16[640,384]{1,0:T(8,128)(2,1)S(1)} %pad_maximum_fusion.3), channel_id=1, source_target_pairs={{0,24},{8,0},{16,8},{24,16},{1,25},{9,1},{17,9},{25,17},{2,26},{10... | collective-permute-start | bytes 1474568 | tf_op jit(solution)/shard_map/ppermute | solution.py:23
  54.2 10.7 %collective-permute-start.6 = (bf16[640,384]{1,0:T(8,128)(2,1)S(1)}, bf16[640,384]{1,0:T(8,128)(2,1)S(1)}, u32[]{:S(2)}, u32[]{:S(2)}) collective-permute-start(bf16[640,384]{1,0:T(8,128)(2,1)S(1)} %pad_maximum_fusion.3), channel_id=1, source_target_pairs={{0,16},{8,24},{16,0},{24,8},{1,17},{9,25},{17,1},{25,9},{2,18},{10... | collective-permute-start | bytes 1474568 | tf_op jit(solution)/shard_map/ppermute | solution.py:23
  54.6 28.3 %collective-permute-start.7 = (bf16[640,384]{1,0:T(8,128)(2,1)S(1)}, bf16[640,384]{1,0:T(8,128)(2,1)S(1)}, u32[]{:S(2)}, u32[]{:S(2)}) collective-permute-start(bf16[640,384]{1,0:T(8,128)(2,1)S(1)} %pad_maximum_fusion.3), channel_id=1, source_target_pairs={{0,8},{8,16},{16,24},{24,0},{1,9},{9,17},{17,25},{25,1},{2,10},{10... | collective-permute-start | bytes 1474568 | tf_op jit(solution)/shard_map/ppermute | solution.py:23
  55.4 30.4 %collective-permute-start.28 = (bf16[640,256]{1,0:T(8,128)(2,1)S(1)}, bf16[640,256]{1,0:T(8,128)(2,1)S(1)}, u32[]{:S(2)}, u32[]{:S(2)}) collective-permute-start(bf16[640,256]{1,0:T(8,128)(2,1)S(1)} %pad_maximum_fusion.7), channel_id=1, source_target_pairs={{0,16},{8,24},{16,0},{24,8},{1,17},{9,25},{17,1},{25,9},{2,18},{10... | collective-permute-start | bytes 983048 | tf_op jit(solution)/shard_map/ppermute | solution.py:23
  64.8 23.5 %collective-permute-start.29 = (bf16[640,256]{1,0:T(8,128)(2,1)S(1)}, bf16[640,256]{1,0:T(8,128)(2,1)S(1)}, u32[]{:S(2)}, u32[]{:S(2)}) collective-permute-start(bf16[640,256]{1,0:T(8,128)(2,1)S(1)} %pad_maximum_fusion.7), channel_id=1, source_target_pairs={{0,8},{8,16},{16,24},{24,0},{1,9},{9,17},{17,25},{25,1},{2,10},{10... | collective-permute-start | bytes 983048 | tf_op jit(solution)/shard_map/ppermute | solution.py:23
  93.2 14.0 %collective-permute-start.12 = (bf16[640,384]{1,0:T(8,128)(2,1)S(1)}, bf16[640,384]{1,0:T(8,128)(2,1)S(1)}, u32[]{:S(2)}, u32[]{:S(2)}) collective-permute-start(bf16[640,384]{1,0:T(8,128)(2,1)S(1)} %pad_maximum_fusion.4), channel_id=1, source_target_pairs={{0,64},{32,96},{64,0},{96,32},{1,65},{33,97},{65,1},{97,33},{2,66}... | collective-permute-start | bytes 1474568 | tf_op jit(solution)/shard_map/ppermute | solution.py:23
  94.1 82.7 %collective-permute-start.30 = (bf16[160,256]{1,0:T(8,128)(2,1)}, bf16[160,256]{1,0:T(8,128)(2,1)}, u32[]{:S(2)}, u32[]{:S(2)}) collective-permute-start(bf16[160,256]{1,0:T(8,128)(2,1)} %get-tuple-element.119), channel_id=1, source_target_pairs={{0,24},{8,0},{16,8},{24,16},{1,25},{9,1},{17,9},{25,17},{2,26},{10... | collective-permute-start | bytes 245768 | tf_op jit(solution)/shard_map/ppermute | solution.py:23
  94.2 14.3 %collective-permute-start.13 = (bf16[640,384]{1,0:T(8,128)(2,1)S(1)}, bf16[640,384]{1,0:T(8,128)(2,1)S(1)}, u32[]{:S(2)}, u32[]{:S(2)}) collective-permute-start(bf16[640,384]{1,0:T(8,128)(2,1)S(1)} %pad_maximum_fusion.4), channel_id=1, source_target_pairs={{0,32},{32,64},{64,96},{96,0},{1,33},{33,65},{65,97},{97,1},{2,34}... | collective-permute-start | bytes 1474568 | tf_op jit(solution)/shard_map/ppermute | solution.py:23
  100.3 76.5 %collective-permute-start.31 = (bf16[160,256]{1,0:T(8,128)(2,1)}, bf16[160,256]{1,0:T(8,128)(2,1)}, u32[]{:S(2)}, u32[]{:S(2)}) collective-permute-start(bf16[160,256]{1,0:T(8,128)(2,1)} %get-tuple-element.119), channel_id=1, source_target_pairs={{0,16},{8,24},{16,0},{24,8},{1,17},{9,25},{17,1},{25,9},{2,18},{10... | collective-permute-start | bytes 245768 | tf_op jit(solution)/shard_map/ppermute | solution.py:23
  131.3 13.7 %collective-permute-start.17 = (bf16[384,128]{1,0:T(8,128)(2,1)S(1)}, bf16[384,128]{1,0:T(8,128)(2,1)S(1)}, u32[]{:S(2)}, u32[]{:S(2)}) collective-permute-start(bf16[384,128]{1,0:T(8,128)(2,1)S(1)} %fusion.95), channel_id=1, source_target_pairs={{0,96},{1,25},{8,104},{9,1},{16,112},{17,9},{24,120},{25,17},{32,0... | collective-permute-start | bytes 294920 | tf_op jit(solution)/shard_map/ppermute | solution.py:42
  133.2 12.3 %collective-permute-start.18 = (bf16[384,128]{1,0:T(8,128)(2,1)S(1)}, bf16[384,128]{1,0:T(8,128)(2,1)S(1)}, u32[]{:S(2)}, u32[]{:S(2)}) collective-permute-start(bf16[384,128]{1,0:T(8,128)(2,1)S(1)} %fusion.95), channel_id=1, source_target_pairs={{0,64},{1,17},{8,72},{9,25},{16,80},{17,1},{24,88},{25,9},{32,96},... | collective-permute-start | bytes 294920 | tf_op jit(solution)/shard_map/ppermute | solution.py:42
  148.7 12.3 %collective-permute-start.22 = (bf16[4,384,128]{2,1,0:T(8,128)(2,1)S(1)}, bf16[4,384,128]{2,1,0:T(8,128)(2,1)S(1)}, u32[]{:S(2)}, u32[]{:S(2)}) collective-permute-start(bf16[4,384,128]{2,1,0:T(8,128)(2,1)S(1)} %pad_maximum_fusion.5), channel_id=1, source_target_pairs={{0,8},{1,33},{8,16},{9,41},{16,24},{17,49},{24,0},{25,57},{32,40},... | collective-permute-start | bytes 1179656 | tf_op jit(solution)/shard_map/ppermute | solution.py:42
  155.5 21.3 %collective-permute-start.32 = (bf16[160,256]{1,0:T(8,128)(2,1)}, bf16[160,256]{1,0:T(8,128)(2,1)}, u32[]{:S(2)}, u32[]{:S(2)}) collective-permute-start(bf16[160,256]{1,0:T(8,128)(2,1)} %get-tuple-element.119), channel_id=1, source_target_pairs={{0,8},{8,16},{16,24},{24,0},{1,9},{9,17},{17,25},{25,1},{2,10},{10... | collective-permute-start | bytes 245768 | tf_op jit(solution)/shard_map/ppermute | solution.py:23
  161.8 40.3 %collective-permute-start.23 = (bf16[16,384,128]{2,1,0:T(8,128)(2,1)}, bf16[16,384,128]{2,1,0:T(8,128)(2,1)}, u32[]{:S(2)}, u32[]{:S(2)}) collective-permute-start(bf16[16,384,128]{2,1,0:T(8,128)(2,1)} %constant_dynamic-update-slice_fusion.14), channel_id=1, source_target_pairs={{0,1},{1,0},{2,3},{3,2},{4,5},{5,4},{6,7},{7,6},{8,9},{9,8},{10,11... | collective-permute-start | bytes 4718600 | tf_op jit(solution)/shard_map/ppermute | solution.py:46
  177.9 11.0 %collective-permute-start.34 = (bf16[640,256]{1,0:T(8,128)(2,1)S(1)}, bf16[640,256]{1,0:T(8,128)(2,1)S(1)}, u32[]{:S(2)}, u32[]{:S(2)}) collective-permute-start(bf16[640,256]{1,0:T(8,128)(2,1)S(1)} %pad_maximum_fusion.8), channel_id=1, source_target_pairs={{0,64},{32,96},{64,0},{96,32},{1,65},{33,97},{65,1},{97,33},{2,66}... | collective-permute-start | bytes 983048 | tf_op jit(solution)/shard_map/ppermute | solution.py:23
  178.6 17.6 %collective-permute-start.35 = (bf16[640,256]{1,0:T(8,128)(2,1)S(1)}, bf16[640,256]{1,0:T(8,128)(2,1)S(1)}, u32[]{:S(2)}, u32[]{:S(2)}) collective-permute-start(bf16[640,256]{1,0:T(8,128)(2,1)S(1)} %pad_maximum_fusion.8), channel_id=1, source_target_pairs={{0,32},{32,64},{64,96},{96,0},{1,33},{33,65},{65,97},{97,1},{2,34}... | collective-permute-start | bytes 983048 | tf_op jit(solution)/shard_map/ppermute | solution.py:23
  232.9 17.7 %collective-permute-start.38 = (bf16[16,384,128]{2,1,0:T(8,128)(2,1)}, bf16[16,384,128]{2,1,0:T(8,128)(2,1)}, u32[]{:S(2)}, u32[]{:S(2)}) collective-permute-start(bf16[16,384,128]{2,1,0:T(8,128)(2,1)} %get-tuple-element.23), channel_id=1, source_target_pairs={{0,1},{1,0},{2,3},{3,2},{4,5},{5,4},{6,7},{7,6},{8,9},{9,8},{10,11... | collective-permute-start | bytes 4718600 | tf_op jit(solution)/shard_map/ppermute | solution.py:46
  252.8 51.2 %collective-permute-start.39 = (bf16[4,384,128]{2,1,0:T(8,128)(2,1)S(1)}, bf16[4,384,128]{2,1,0:T(8,128)(2,1)S(1)}, u32[]{:S(2)}, u32[]{:S(2)}) collective-permute-start(bf16[4,384,128]{2,1,0:T(8,128)(2,1)S(1)} %get-tuple-element.61), channel_id=1, source_target_pairs={{0,8},{1,33},{8,16},{9,41},{16,24},{17,49},{24,0},{25,57},{32,40},... | collective-permute-start | bytes 1179656 | tf_op jit(solution)/shard_map/ppermute | solution.py:42
  267.4 42.1 %collective-permute-start.40 = (bf16[4,384,128]{2,1,0:T(8,128)(2,1)S(1)}, bf16[4,384,128]{2,1,0:T(8,128)(2,1)S(1)}, u32[]{:S(2)}, u32[]{:S(2)}) collective-permute-start(bf16[4,384,128]{2,1,0:T(8,128)(2,1)S(1)} %get-tuple-element.63), channel_id=1, source_target_pairs={{0,16},{1,65},{8,24},{9,73},{16,0},{17,81},{24,8},{25,89},{32,48},... | collective-permute-start | bytes 1179656 | tf_op jit(solution)/shard_map/ppermute | solution.py:42
  309.7 17.7 %collective-permute-start.42 = (bf16[384,128]{1,0:T(8,128)(2,1)S(1)}, bf16[384,128]{1,0:T(8,128)(2,1)S(1)}, u32[]{:S(2)}, u32[]{:S(2)}) collective-permute-start(bf16[384,128]{1,0:T(8,128)(2,1)S(1)} %get-tuple-element.98), channel_id=1, source_target_pairs={{0,32},{1,9},{8,40},{9,17},{16,48},{17,25},{24,56},{25,1},{32,64},... | collective-permute-start | bytes 294920 | tf_op jit(solution)/shard_map/ppermute | solution.py:42
  312.0 16.1 %collective-permute-start.43 = (bf16[384,128]{1,0:T(8,128)(2,1)S(1)}, bf16[384,128]{1,0:T(8,128)(2,1)S(1)}, u32[]{:S(2)}, u32[]{:S(2)}) collective-permute-start(bf16[384,128]{1,0:T(8,128)(2,1)S(1)} %get-tuple-element.100), channel_id=1, source_target_pairs={{0,64},{1,17},{8,72},{9,25},{16,80},{17,1},{24,88},{25,9},{32,96},... | collective-permute-start | bytes 294920 | tf_op jit(solution)/shard_map/ppermute | solution.py:42
  334.6 15.5 %collective-permute-start.55 = (bf16[640,256]{1,0:T(8,128)(2,1)}, bf16[640,256]{1,0:T(8,128)(2,1)}, u32[]{:S(2)}, u32[]{:S(2)}) collective-permute-start(bf16[640,256]{1,0:T(8,128)(2,1)} %get-tuple-element.52), channel_id=1, source_target_pairs={{0,8},{8,16},{16,24},{24,0},{1,9},{9,17},{17,25},{25,1},{2,10},{10... | collective-permute-start | bytes 983048 | tf_op jit(solution)/shard_map/ppermute | solution.py:27
  335.2 19.8 %collective-permute-start.56 = (bf16[640,256]{1,0:T(8,128)(2,1)}, bf16[640,256]{1,0:T(8,128)(2,1)}, u32[]{:S(2)}, u32[]{:S(2)}) collective-permute-start(bf16[640,256]{1,0:T(8,128)(2,1)} %get-tuple-element.57), channel_id=1, source_target_pairs={{0,16},{8,24},{16,0},{24,8},{1,17},{9,25},{17,1},{25,9},{2,18},{10... | collective-permute-start | bytes 983048 | tf_op jit(solution)/shard_map/ppermute | solution.py:27
  338.8 17.5 %collective-permute-start.57 = (bf16[640,256]{1,0:T(8,128)(2,1)}, bf16[640,256]{1,0:T(8,128)(2,1)}, u32[]{:S(2)}, u32[]{:S(2)}) collective-permute-start(bf16[640,256]{1,0:T(8,128)(2,1)} %get-tuple-element.56), channel_id=1, source_target_pairs={{0,24},{8,0},{16,8},{24,16},{1,25},{9,1},{17,9},{25,17},{2,26},{10... | collective-permute-start | bytes 983048 | tf_op jit(solution)/shard_map/ppermute | solution.py:27
  338.9 17.4 %collective-permute-start.67 = (bf16[640,256]{1,0:T(8,128)(2,1)}, bf16[640,256]{1,0:T(8,128)(2,1)}, u32[]{:S(2)}, u32[]{:S(2)}) collective-permute-start(bf16[640,256]{1,0:T(8,128)(2,1)} %get-tuple-element.55), channel_id=1, source_target_pairs={{0,32},{32,64},{64,96},{96,0},{1,33},{33,65},{65,97},{97,1},{2,34}... | collective-permute-start | bytes 983048 | tf_op jit(solution)/shard_map/ppermute | solution.py:27
  338.9 17.4 %collective-permute-start.68 = (bf16[640,256]{1,0:T(8,128)(2,1)}, bf16[640,256]{1,0:T(8,128)(2,1)}, u32[]{:S(2)}, u32[]{:S(2)}) collective-permute-start(bf16[640,256]{1,0:T(8,128)(2,1)} %get-tuple-element.54), channel_id=1, source_target_pairs={{0,64},{32,96},{64,0},{96,32},{1,65},{33,97},{65,1},{97,33},{2,66}... | collective-permute-start | bytes 983048 | tf_op jit(solution)/shard_map/ppermute | solution.py:27
  355.0 23.4 %collective-permute-start.49 = (bf16[640,384]{1,0:T(8,128)(2,1)S(1)}, bf16[640,384]{1,0:T(8,128)(2,1)S(1)}, u32[]{:S(2)}, u32[]{:S(2)}) collective-permute-start(bf16[640,384]{1,0:T(8,128)(2,1)S(1)} %get-tuple-element.32), channel_id=1, source_target_pairs={{0,8},{8,16},{16,24},{24,0},{1,9},{9,17},{17,25},{25,1},{2,10},{10... | collective-permute-start | bytes 1474568 | tf_op jit(solution)/shard_map/ppermute | solution.py:27
  356.3 24.9 %collective-permute-start.50 = (bf16[640,384]{1,0:T(8,128)(2,1)S(1)}, bf16[640,384]{1,0:T(8,128)(2,1)S(1)}, u32[]{:S(2)}, u32[]{:S(2)}) collective-permute-start(bf16[640,384]{1,0:T(8,128)(2,1)S(1)} %get-tuple-element.37), channel_id=1, source_target_pairs={{0,16},{8,24},{16,0},{24,8},{1,17},{9,25},{17,1},{25,9},{2,18},{10... | collective-permute-start | bytes 1474568 | tf_op jit(solution)/shard_map/ppermute | solution.py:27
  364.5 12.1 %collective-permute-start.70 = (bf16[160,256]{1,0:T(8,128)(2,1)S(1)}, bf16[160,256]{1,0:T(8,128)(2,1)S(1)}, u32[]{:S(2)}, u32[]{:S(2)}) collective-permute-start(bf16[160,256]{1,0:T(8,128)(2,1)S(1)} %get-tuple-element.110), channel_id=1, source_target_pairs={{0,8},{8,16},{16,24},{24,0},{1,9},{9,17},{17,25},{25,1},{2,10},{10... | collective-permute-start | bytes 245768 | tf_op jit(solution)/shard_map/ppermute | solution.py:27
  366.6 11.8 %collective-permute-start.71 = (bf16[160,256]{1,0:T(8,128)(2,1)S(1)}, bf16[160,256]{1,0:T(8,128)(2,1)S(1)}, u32[]{:S(2)}, u32[]{:S(2)}) collective-permute-start(bf16[160,256]{1,0:T(8,128)(2,1)S(1)} %get-tuple-element.112), channel_id=1, source_target_pairs={{0,16},{8,24},{16,0},{24,8},{1,17},{9,25},{17,1},{25,9},{2,18},{10... | collective-permute-start | bytes 245768 | tf_op jit(solution)/shard_map/ppermute | solution.py:27
  367.4 11.0 %collective-permute-start.72 = (bf16[160,256]{1,0:T(8,128)(2,1)S(1)}, bf16[160,256]{1,0:T(8,128)(2,1)S(1)}, u32[]{:S(2)}, u32[]{:S(2)}) collective-permute-start(bf16[160,256]{1,0:T(8,128)(2,1)S(1)} %get-tuple-element.111), channel_id=1, source_target_pairs={{0,24},{8,0},{16,8},{24,16},{1,25},{9,1},{17,9},{25,17},{2,26},{10... | collective-permute-start | bytes 245768 | tf_op jit(solution)/shard_map/ppermute | solution.py:27
  376.6 10.9 %collective-permute-start.51 = (bf16[640,384]{1,0:T(8,128)(2,1)S(1)}, bf16[640,384]{1,0:T(8,128)(2,1)S(1)}, u32[]{:S(2)}, u32[]{:S(2)}) collective-permute-start(bf16[640,384]{1,0:T(8,128)(2,1)S(1)} %get-tuple-element.36), channel_id=1, source_target_pairs={{0,24},{8,0},{16,8},{24,16},{1,25},{9,1},{17,9},{25,17},{2,26},{10... | collective-permute-start | bytes 1474568 | tf_op jit(solution)/shard_map/ppermute | solution.py:27
  378.4 22.6 %collective-permute-start.61 = (bf16[640,384]{1,0:T(8,128)(2,1)S(1)}, bf16[640,384]{1,0:T(8,128)(2,1)S(1)}, u32[]{:S(2)}, u32[]{:S(2)}) collective-permute-start(bf16[640,384]{1,0:T(8,128)(2,1)S(1)} %get-tuple-element.35), channel_id=1, source_target_pairs={{0,32},{32,64},{64,96},{96,0},{1,33},{33,65},{65,97},{97,1},{2,34}... | collective-permute-start | bytes 1474568 | tf_op jit(solution)/shard_map/ppermute | solution.py:27
  378.4 22.6 %collective-permute-start.62 = (bf16[640,384]{1,0:T(8,128)(2,1)S(1)}, bf16[640,384]{1,0:T(8,128)(2,1)S(1)}, u32[]{:S(2)}, u32[]{:S(2)}) collective-permute-start(bf16[640,384]{1,0:T(8,128)(2,1)S(1)} %get-tuple-element.34), channel_id=1, source_target_pairs={{0,64},{32,96},{64,0},{96,32},{1,65},{33,97},{65,1},{97,33},{2,66}... | collective-permute-start | bytes 1474568 | tf_op jit(solution)/shard_map/ppermute | solution.py:27
  378.4 23.1 %collective-permute-start.63 = (bf16[640,384]{1,0:T(8,128)(2,1)S(1)}, bf16[640,384]{1,0:T(8,128)(2,1)S(1)}, u32[]{:S(2)}, u32[]{:S(2)}) collective-permute-start(bf16[640,384]{1,0:T(8,128)(2,1)S(1)} %get-tuple-element.33), channel_id=1, source_target_pairs={{0,96},{32,0},{64,32},{96,64},{1,97},{33,1},{65,33},{97,65},{2,98}... | collective-permute-start | bytes 1474568 | tf_op jit(solution)/shard_map/ppermute | solution.py:27
  381.1 43.2 %collective-permute-start.45 = (bf16[4,192,1280]{2,1,0:T(8,128)(2,1)S(1)}, bf16[4,192,1280]{2,1,0:T(8,128)(2,1)S(1)}, u32[]{:S(2)}, u32[]{:S(2)}) collective-permute-start(bf16[4,192,1280]{2,1,0:T(8,128)(2,1)S(1)} %broadcast_select_fusion), channel_id=1, source_target_pairs={{0,1},{1,0},{2,3},{3,2},{4,5},{5,4},{6,7},{7,6},{8,9},{9,8},{10,11... | collective-permute-start | bytes 5898248 | tf_op jit(solution)/shard_map/ppermute | solution.py:46
  387.5 37.9 %collective-permute-start.36 = (bf16[192,512]{1,0:T(8,128)(2,1)S(1)}, bf16[192,512]{1,0:T(8,128)(2,1)S(1)}, u32[]{:S(2)}, u32[]{:S(2)}) collective-permute-start(bf16[192,512]{1,0:T(8,128)(2,1)S(1)} %get-tuple-element.27), channel_id=1, source_target_pairs={{1,4},{4,1},{3,6},{6,3},{9,12},{12,9},{11,14},{14,11},{17,20},{20,... | collective-permute-start | bytes 589832 | tf_op jit(solution)/shard_map/ppermute | solution.py:66
  416.7 12.1 %collective-permute-start.37 = (bf16[192,512]{1,0:T(8,128)(2,1)S(1)}, bf16[192,512]{1,0:T(8,128)(2,1)S(1)}, u32[]{:S(2)}, u32[]{:S(2)}) collective-permute-start(bf16[192,512]{1,0:T(8,128)(2,1)S(1)} %get-tuple-element.26), channel_id=1, source_target_pairs={{1,0},{4,5},{5,1},{0,4},{3,2},{6,7},{7,3},{2,6},{9,8},{12,13},{13,... | collective-permute-start | bytes 589832 | tf_op jit(solution)/shard_map/ppermute | solution.py:65
  420.8 10.8 %collective-permute-start.73 = (bf16[160,640]{1,0:T(8,128)(2,1)S(1)}, bf16[160,640]{1,0:T(8,128)(2,1)S(1)}, u32[]{:S(2)}, u32[]{:S(2)}) collective-permute-start(bf16[160,640]{1,0:T(8,128)(2,1)S(1)} %get-tuple-element.22), channel_id=1, source_target_pairs={{1,4},{4,1},{3,6},{6,3},{9,12},{12,9},{11,14},{14,11},{17,20},{20,... | collective-permute-start | bytes 614408 | tf_op jit(solution)/shard_map/ppermute | solution.py:66
  425.3 13.4 %collective-permute-start.46 = (bf16[192,1280]{1,0:T(8,128)(2,1)S(1)}, bf16[192,1280]{1,0:T(8,128)(2,1)S(1)}, u32[]{:S(2)}, u32[]{:S(2)}) collective-permute-start(bf16[192,1280]{1,0:T(8,128)(2,1)S(1)} %get-tuple-element.58), channel_id=1, source_target_pairs={{0,4},{4,2},{2,6},{6,0},{1,5},{5,3},{3,7},{7,1},{8,12},{12,10},{10... | collective-permute-start | bytes 1474568 | tf_op jit(solution)/shard_map/ppermute | solution.py:417
  425.4 25.6 %collective-permute-start.47 = (bf16[192,1280]{1,0:T(8,128)(2,1)S(1)}, bf16[192,1280]{1,0:T(8,128)(2,1)S(1)}, u32[]{:S(2)}, u32[]{:S(2)}) collective-permute-start(bf16[192,1280]{1,0:T(8,128)(2,1)S(1)} %get-tuple-element.60), channel_id=1, source_target_pairs={{0,2},{4,6},{2,0},{6,4},{1,3},{5,7},{3,1},{7,5},{8,10},{12,14},{10... | collective-permute-start | bytes 1474568 | tf_op jit(solution)/shard_map/ppermute | solution.py:417
  428.8 22.2 %collective-permute-start.48 = (bf16[192,1280]{1,0:T(8,128)(2,1)S(1)}, bf16[192,1280]{1,0:T(8,128)(2,1)S(1)}, u32[]{:S(2)}, u32[]{:S(2)}) collective-permute-start(bf16[192,1280]{1,0:T(8,128)(2,1)S(1)} %get-tuple-element.59), channel_id=1, source_target_pairs={{0,6},{4,0},{2,4},{6,2},{1,7},{5,1},{3,5},{7,3},{8,14},{12,8},{10,... | collective-permute-start | bytes 1474568 | tf_op jit(solution)/shard_map/ppermute | solution.py:417
  (43 other events, 526.7 us)
